TPU v7x, 256 devices: a whole 4x4x8 slice. The times are simulated.
256 devices in a mesh: expert: 64 (over z, y, x_hi), dp: 4 (over x_lo, core).
Axes of the slice: x: 4 (x_hi: 2, x_lo: 2; x = x_hi * 2 + x_lo), y: 4, z: 8, core: 2. Of those that a mesh axis runs over, the one named last changes fastest.
Arguments:
- tokens: bfloat16 [3072, 7168], P(('expert', 'dp')), may hold values from -6 to 6
- expert_ids: int32 [3072, 8], P(('expert', 'dp')), may hold values from 0 to 63, all different within a row; in each aligned block of 12 rows (0 to 11, 12 to 23, ...) at most 2 rows name the same one
- gates: bfloat16 [3072, 8], P(('expert', 'dp')), may hold values from 0.049804688 to 1
- w_gate: bfloat16 [64, 7168, 1024], P('expert', None, 'dp'), may hold values from -0.0625 to 0.0625
- w_up: bfloat16 [64, 7168, 1024], P('expert', None, 'dp'), may hold values from -0.0625 to 0.0625
- w_down: bfloat16 [64, 1024, 7168], P('expert', 'dp'), may hold values from -0.1875 to 0.1875
Outputs:
- mixed_out: bfloat16 [3072, 7168], P(('expert', 'dp'))
Inputs may be any that keep to these rules, and one draw needn't show every extreme that they name: `expert_ids`: each row names 8 different experts. Within the rows of one device (aligned blocks of 12 rows) no expert is named by more than 2 rows, a bound that some block reaches of some device in every draw.
All inputs are finite; a program needn't handle non-finite values.
Results may differ from a plain program's by a relative error of at most 0.015.
Values may be sent and summed in bfloat16 or wider, within the bound.
A program may use at most 128 MiB of HBM per device.

v0:
```python
import jax
import jax.numpy as jnp
from jax import lax
from jax.sharding import PartitionSpec as P

CAP = 2


def slot_numbers(route_ids, experts):
    onehot = (route_ids[:, None] == jnp.arange(experts, dtype=jnp.int32)[None, :]).astype(jnp.int32)
    before = jnp.cumsum(onehot, axis=0) - onehot
    return jnp.sum(before * onehot, axis=1)


def local(tokens, expert_ids, gates, w_gate, w_up, w_down):
    tok_rows, model_width = tokens.shape
    topk = expert_ids.shape[1]
    local_count = w_gate.shape[0]
    owners = lax.axis_size("expert")
    groups = lax.axis_size("dp")
    experts = local_count * owners
    capacity = CAP
    members = (
        lax.all_gather(tokens, "dp", axis=0, tiled=True),
        lax.all_gather(expert_ids, "dp", axis=0, tiled=True),
        lax.all_gather(gates, "dp", axis=0, tiled=True),
    )
    all_tokens, all_ids, all_gates = members
    member_ids = all_ids.reshape(groups, tok_rows * topk)
    slot_index = jax.vmap(lambda one_row: slot_numbers(one_row, experts))(member_ids)
    member = jnp.arange(groups, dtype=jnp.int32)[:, None]
    position = (member_ids * (groups * capacity) + member * capacity + slot_index).reshape(
        groups * tok_rows, topk
    )
    columns = jnp.arange(experts * groups * capacity, dtype=jnp.int32)
    matches = position[:, :, None] == columns[None, None, :]
    select = jnp.any(matches, axis=1).astype(jnp.bfloat16)
    outbound = jnp.einsum(
        "tp,td->pd", select, all_tokens, preferred_element_type=jnp.float32
    ).astype(jnp.bfloat16)
    outbound = outbound.reshape(owners, local_count, groups * capacity, model_width)
    row_block = lax.all_to_all(outbound, "expert", split_axis=0, concat_axis=0, tiled=True)
    gate_out = jnp.einsum("send,edh->senh", row_block, w_gate, preferred_element_type=jnp.float32)
    up_out = jnp.einsum("send,edh->senh", row_block, w_up, preferred_element_type=jnp.float32)
    hidden = (jax.nn.silu(gate_out) * up_out).astype(jnp.bfloat16)
    partial_value = lax.all_to_all(
        jnp.einsum("senh,ehd->send", hidden, w_down, preferred_element_type=jnp.float32).astype(
            jnp.bfloat16
        ),
        "expert",
        split_axis=0,
        concat_axis=0,
        tiled=True,
    )
    weight_map = jnp.sum(
        jnp.where(matches, all_gates[:, :, None].astype(jnp.float32), 0.0), axis=1
    ).astype(jnp.bfloat16)
    partial_term = jnp.dot(
        weight_map, partial_value.reshape(-1, model_width), preferred_element_type=jnp.float32
    )
    mixed_out = lax.psum_scatter(
        partial_term.astype(jnp.bfloat16), "dp", scatter_dimension=0, tiled=True
    )
    return mixed_out


def solution(mesh):
    in_specs = (
        P(("expert", "dp"), None),
        P(("expert", "dp"), None),
        P(("expert", "dp"), None),
        P("expert", None, "dp"),
        P("expert", None, "dp"),
        P("expert", "dp", None),
    )
    out_specs = P(("expert", "dp"), None)
    return jax.shard_map(local, mesh=mesh, in_specs=in_specs, out_specs=out_specs, check_vma=False)
```

profile of v0, /device:TPU:6, one launch (start us, length us, event | category | flops | bytes accessed | tf_op | source)
XLA Modules:
  0.0 414.1 jit_solution(8068163804220310635)
XLA Ops:
  0.0 5.3 %all-gather = s32[4,12,8]{1,2,0:T(8,128)S(1)} all-gather(s32[1,12,8]{1,2,0:T(8,128)} %bitcast.94), channel_id=1, replica_groups=mesh['expert'=64,'dp'=4] {'dp'}, dimensions={0}, use_global_device_ids=true | all-gather | bytes 1920 | tf_op jit(solution)/shard_map/all_gather | solution.py:25
  5.3 0.1 copy.22
  5.4 0.1 eq.28
  5.5 0.1 fusion.47
  5.6 0.2 reduce_window_sum.11
  5.8 0.2 select_reduce_fusion.1
  6.1 0.1 reduce_sum.21
  6.1 0.1 copy.23
  6.2 0.1 reshape.59
  6.3 0.1 add.25
  6.4 0.1 add.26
  6.5 0.1 copy.24
  6.6 0.3 fusion.36
  6.9 9.6 %all-gather.2 = bf16[4,12,7168]{2,1,0:T(8,128)(2,1)S(1)} all-gather(bf16[1,12,7168]{2,1,0:T(8,128)(2,1)} %bitcast.93), channel_id=1, replica_groups=mesh['expert'=64,'dp'=4] {'dp'}, dimensions={0}, use_global_device_ids=true | all-gather | bytes 860160 | tf_op jit(solution)/shard_map/all_gather | solution.py:24
  16.5 0.2 reshape.55
  16.7 2.1 fusion.1
  18.8 0.0 copy-start.3
  18.8 177.9 %all_to_all.10 = bf16[64,1,8,7168]{3,2,1,0:T(8,128)(2,1)S(1)} all-to-all(bf16[64,1,8,7168]{3,2,1,0:T(8,128)(2,1)S(1)} %fusion.1), channel_id=1, replica_groups=mesh['expert'=64,'dp'=4] {'expert'}, dimensions={0} | all-to-all | bytes 14680064 | tf_op jit(solution)/shard_map/all_to_all | solution.py:42
  196.7 0.0 copy-start
  196.7 3.0 copy-done
  199.7 0.0 copy-done.3
  199.7 2.1 fusion.11
  201.8 15.9 %fusion.2 = bf16[64,1,8,7168]{3,2,1,0:T(8,128)(2,1)} fusion(bf16[1,256,7168]{2,1,0:T(8,128)(2,1)} %param.11, bf16[1,7168,256]{2,1,0:T(8,128)(2,1)} %param.10, bf16[64,1,8,7168]{3,2,1,0:T(8,128)(2,1)} %copy-done, f32[64,1,8,256]{3,2,0,1:T(8,128)S(1)} %fusion.11), kind=kOutput, calls=%fused_computation.3 | convolution fusion | flops 3762552832 | bytes 22544384 | tf_op jit(solution)/shard_map/senh,ehd->send/dot_general | solution.py:47
  217.7 0.0 copy-start.1
  217.7 8.6 %all-to-all-start.1 = ((bf16[64,1,8,7168]{3,2,1,0:T(8,128)(2,1)}), bf16[64,1,8,7168]{3,2,1,0:T(8,128)(2,1)}, u32[]{:S(2)}, u32[]{:S(2)}) async-start(bf16[64,1,8,7168]{3,2,1,0:T(8,128)(2,1)} %fusion.2), calls=%async_computation.1 | async-start | bytes 14680064 | tf_op jit(solution)/shard_map/all_to_all | solution.py:46
  226.4 0.0 copy-start.2
  226.4 0.0 copy-done.1
  226.4 19.0 %all-gather.1 = bf16[4,12,8]{1,2,0:T(8,128)(2,1)S(1)} all-gather(bf16[1,12,8]{1,2,0:T(8,128)(2,1)S(1)} %bitcast.95), channel_id=1, replica_groups=mesh['expert'=64,'dp'=4] {'dp'}, dimensions={0}, use_global_device_ids=true | all-gather | bytes 960 | tf_op jit(solution)/shard_map/all_gather | solution.py:26
  245.4 0.1 reshape.56
  245.5 0.1 copy.26
  245.5 0.3 select_reduce_fusion
  245.9 142.5 %all-to-all-done.1 = bf16[64,1,8,7168]{3,2,1,0:T(8,128)(2,1)} async-done(((bf16[64,1,8,7168]{3,2,1,0:T(8,128)(2,1)}), bf16[64,1,8,7168]{3,2,1,0:T(8,128)(2,1)}, u32[]{:S(2)}, u32[]{:S(2)}) %all-to-all-start.1) | async-done | bytes 7340064 | tf_op jit(solution)/shard_map/all_to_all | solution.py:46
  388.3 4.5 %convolution_convert_fusion.2 = bf16[48,7168]{1,0:T(8,128)(2,1)S(1)} fusion(bf16[64,1,8,7168]{3,2,1,0:T(8,128)(2,1)} %all-to-all-done.1, bf16[48,512]{1,0:T(8,128)(2,1)S(1)} %select_reduce_fusion), kind=kOutput, calls=%fused_computation.4 | convolution fusion | flops 352665600 | bytes 8077312 | tf_op jit(solution)/shard_map/dot_general | solution.py:58
  392.8 12.5 %fusion = bf16[16,7168]{1,0:T(8,128)(2,1)S(1)} fusion(bf16[48,7168]{1,0:T(8,128)(2,1)S(1)} %convolution_convert_fusion.2), kind=kCustom, calls=%all-reduce-scatter | all-reduce-scatter fusion | flops 458753 | bytes 918528
  405.3 0.1 slice
  405.4 1.9 collective-permute-start
  407.3 0.0 copy-done.2
  407.3 0.6 dynamic-slice.4
  408.6 4.2 %collective-permute-done = bf16[12,7168]{1,0:T(8,128)(2,1)S(1)} collective-permute-done((bf16[12,7168]{1,0:T(8,128)(2,1)S(1)}, bf16[12,7168]{1,0:T(8,128)(2,1)S(1)}, u32[]{:S(2)}, u32[]{:S(2)}) %collective-permute-start) | collective-permute-done | bytes 172064
  412.7 0.6 concatenate
  413.4 0.8 constant_dynamic-slice_fusion
  (5 shorter events, 0.0 us)
Async XLA Ops:
  18.8 181.0 %copy-start.3 = (bf16[1,7168,256]{2,1,0:T(8,128)(2,1)S(1)}, bf16[1,7168,256]{2,1,0:T(8,128)(2,1)}, u32[]{:S(2)}) copy-start(bf16[1,7168,256]{2,1,0:T(8,128)(2,1)} %param.9) | copy-start | bytes 11010052
  196.7 3.0 copy-start
  217.7 8.6 %copy-start.1 = (bf16[12,8]{0,1:T(8,128)(2,1)S(1)}, bf16[12,8]{0,1:T(8,128)(2,1)}, u32[]{:S(2)}) copy-start(bf16[12,8]{0,1:T(8,128)(2,1)} %param.8) | copy-start | bytes 580
  217.7 170.6 %all-to-all-start.1 = ((bf16[64,1,8,7168]{3,2,1,0:T(8,128)(2,1)}), bf16[64,1,8,7168]{3,2,1,0:T(8,128)(2,1)}, u32[]{:S(2)}, u32[]{:S(2)}) async-start(bf16[64,1,8,7168]{3,2,1,0:T(8,128)(2,1)} %fusion.2), calls=%async_computation.1 | async-start | bytes 14680064 | tf_op jit(solution)/shard_map/all_to_all | solution.py:46
  226.4 180.9 %copy-start.2 = (u32[256]{0:T(256)S(1)}, u32[256]{0:T(256)}, u32[]{:S(2)}) copy-start(u32[256]{0:T(256)} %constant.25) | copy-start | bytes 3076
  405.4 7.3 %collective-permute-start = (bf16[12,7168]{1,0:T(8,128)(2,1)S(1)}, bf16[12,7168]{1,0:T(8,128)(2,1)S(1)}, u32[]{:S(2)}, u32[]{:S(2)}) collective-permute-start(bf16[12,7168]{1,0:T(8,128)(2,1)S(1)} %slice), channel_id=1, source_target_pairs={{0,1},{1,2},{2,3},{4,5},{5,6},{6,7},{8,9},{9,10},{10,11},{12,13},{... | collective-permute-start | bytes 516104
where the time goes:
time: 414 us
  blocking collectives  224 us (54%)
  waiting for transfers between devices  147 us (36%)
  matrix products  24.6 us (6%)
  starting transfers between devices  10.5 us (3%)
  local copies, waits for them, and re-layouts  6.08 us (1%)
    all_to_all x1, blocking collectives, local(): lax.all_to_all(outbound, 'expert', split_axis=0, concat_axis=0, tiled=True)  178 us
    all_to_all x1, waiting for transfers between devices, local(): lax.all_to_all(jnp.einsum('senh,ehd->send', hidden, w_down, preferred_ele...  142 us
    all_gather x1, blocking collectives, local(): lax.all_gather(gates, 'dp', axis=0, tiled=True)  19 us
    dot_general x1, matrix products, local(): jnp.einsum('senh,ehd->send', hidden, w_down, preferred_element_type=jnp.f...  15.9 us
    unnamed x1, blocking collectives  12.5 us
    all_gather x1, blocking collectives, local(): lax.all_gather(tokens, 'dp', axis=0, tiled=True)  9.6 us
    all_to_all x1, starting transfers between devices, local(): lax.all_to_all(jnp.einsum('senh,ehd->send', hidden, w_down, preferred_ele...  8.62 us
  transfers between devices with their start and end apart: 2, of which 2 were waited for; matrix products, arithmetic and copies ran while one was open for 0% of the time, Pallas kernels for 0%

commit v1 on v0

v1 whole, which is shorter than its diff:
```python
import functools

import jax
import jax.numpy as jnp
from jax import lax
from jax.experimental import pallas as pl
from jax.experimental.pallas import tpu as pltpu
from jax.sharding import PartitionSpec as P

CAP = 2
PAD = 16
YS = 4
CHUNK = 1024
MESH = pl.DeviceIdType.MESH


def dot(a, b):
    return jnp.dot(a, b, preferred_element_type=jnp.float32)


def kernel(
    zs, ys, n, width,
    tok_ref, ids_ref, gates_ref, wg_hbm, wu_hbm, wd_hbm, out_ref,
    ids16, gates16, mtsend, mtbuf, sel, zbuf, slot, rows, wg, wu, wd, acc_g, acc_u, hid,
    send_c, recv_c, send_x, recv_x, ret, retr, zsend, zrecv,
    w_sem, mt_sem, z_s, z_r, p_s, p_r, c_s, c_r, o_s, o_r, k_s, k_r,
    rc_s, rc_r, rx_s, rx_r, rp_s, rp_r, rz_s, rz_r,
):
    e = lax.axis_index("expert")
    q = lax.axis_index("dp")
    js = 2 * ys
    z, j = e // js, e % js
    y, xh = j // 2, j % 2
    xl, core = q // 2, q % 2
    tok_rows, topk = ids_ref.shape
    lanes = js * zs * CAP

    planes = []
    for dy in range(ys):
        for dx in range(2):
            if dy or dx:
                there = ((y + dy) % ys) * 2 + (xh + dx) % 2
                group = q if dx == 0 else (1 - xl) * 2 + core
                planes.append(((z * js + there, group), there, group))
    columns = []
    for dz in range(1, zs):
        there = (z + dz) % zs
        columns.append(((there * js + j, q), there))
    mate_q = xl * 2 + (1 - core)
    opp_q = (1 - xl) * 2 + core
    far_q = (1 - xl) * 2 + (1 - core)
    mate, opp = (e, mate_q), (e, opp_q)

    barrier = pltpu.get_barrier_semaphore()
    partners = [p[0] for p in planes] + [c[0] for c in columns] + [mate, opp]
    for partner in partners:
        pl.semaphore_signal(barrier, inc=1, device_id=partner, device_id_type=MESH)

    weights = [
        pltpu.make_async_copy(wg_hbm.at[0], wg, w_sem.at[0]),
        pltpu.make_async_copy(wu_hbm.at[0], wu, w_sem.at[1]),
    ] + [
        pltpu.make_async_copy(wd_hbm.at[0, :, pl.ds(c * width, width)], wd.at[c], w_sem.at[2 + c])
        for c in range(n)
    ]
    for copy in weights:
        copy.start()

    def remote(src, dst, send, recv, device):
        return pltpu.make_async_remote_copy(
            src_ref=src, dst_ref=dst, send_sem=send, recv_sem=recv,
            device_id=device, device_id_type=MESH,
        )

    ids16[...] = jnp.full(ids16.shape, -1, jnp.int32)
    ids16[0:tok_rows, :] = ids_ref[...]
    gates16[...] = jnp.zeros(gates16.shape, jnp.float32)
    gates16[0:tok_rows, :] = gates_ref[...].astype(jnp.float32)
    lane = lax.broadcasted_iota(jnp.int32, (PAD, lanes), 1)
    lane_expert = lane // (zs * CAP)
    lane_mine = (lane // CAP) % zs == z
    lane_slot = (lane % CAP).astype(jnp.float32)
    lower = (
        lax.broadcasted_iota(jnp.int32, (PAD, PAD), 0) > lax.broadcasted_iota(jnp.int32, (PAD, PAD), 1)
    ).astype(jnp.float32)
    for plane in range(zs):
        named = jnp.zeros((PAD, lanes), jnp.float32)
        weight = jnp.zeros((PAD, lanes), jnp.float32)
        for k in range(topk):
            match = ids16[:, k:k + 1] == lane_expert + plane * js
            named = named + jnp.where(match, 1.0, 0.0)
            weight = weight + jnp.where(match, gates16[:, k:k + 1], 0.0)
        before = dot(lower, named)
        mtsend[plane] = jnp.where((before == lane_slot) & lane_mine, weight, 0.0).astype(jnp.bfloat16)
    mtbuf[z] = mtsend[z]
    for c in range(n):
        zbuf[c, z] = jnp.zeros((PAD, width), jnp.bfloat16)
        zbuf[c, z, 0:tok_rows, :] = tok_ref[:, c * width:(c + 1) * width]

    pl.semaphore_wait(barrier, len(partners))

    for device, there in columns:
        remote(mtsend.at[there], mtbuf.at[z], mt_sem.at[0], mt_sem.at[1], device).start()

    def start_columns(c):
        for device, _ in columns:
            remote(zbuf.at[c, z], zbuf.at[c, z], z_s.at[c], z_r.at[c], device).start()

    for c in range(n):
        start_columns(c)

    acc_g[...] = jnp.zeros_like(acc_g)
    acc_u[...] = jnp.zeros_like(acc_u)
    all_mt = mtbuf.at[pl.ds(0, zs - 1)]
    all_mts = mtsend.at[pl.ds(0, zs - 1)]
    remote(all_mts, all_mt, mt_sem.at[0], mt_sem.at[1], mate).wait_recv()
    mixing = mtbuf[...].reshape(zs * PAD, lanes)
    sel[...] = jnp.where(mixing.astype(jnp.float32) != 0.0, 1.0, 0.0).T.astype(jnp.bfloat16)

    def wait_columns(buf, c, send, recv):
        part = buf.at[c, pl.ds(0, zs - 1)]
        return remote(part, part, send.at[c], recv.at[c], mate)

    def wait_planes(buf, c, send, recv):
        part = buf.at[c, pl.ds(0, js - 1)]
        return remote(part, part, send.at[c], recv.at[c], mate)

    def to_mate(c):
        return remote(rows.at[c, q], rows.at[c, q], c_s.at[c], c_r.at[c], mate)

    def to_opp(c):
        return remote(rows.at[c, q], rows.at[c, q], o_s.at[c], o_r.at[c], opp)

    def pass_on(c):
        return remote(rows.at[c, opp_q], rows.at[c, opp_q], k_s.at[c], k_r.at[c], mate)

    def dispatch(s, carry):
        @pl.when(s < n)
        def _():
            c = s
            wait_columns(zbuf, c, z_s, z_r).wait_recv()
            chosen = dot(sel[...], zbuf[c].reshape(zs * PAD, width)).astype(jnp.bfloat16)
            slot[c] = chosen.reshape(js, zs * CAP, width)
            for device, there, group in planes:
                remote(slot.at[c, there], rows.at[c, group, j], p_s.at[c], p_r.at[c], device).start()
            rows[c, q, j] = slot[c, j]

        @pl.when((s >= 1) & (s < n + 1))
        def _():
            c = s - 1
            wait_planes(slot, c, p_s, p_r).wait_recv()
            to_opp(c).start()
            to_mate(c).start()

        @pl.when((s >= 2) & (s < n + 2))
        def _():
            c = s - 2
            to_opp(c).wait_recv()
            pass_on(c).start()

        @pl.when(s == 3)
        def _():
            weights[0].wait()
            weights[1].wait()

        @pl.when(s >= 3)
        def _():
            c = s - 3
            to_mate(c).wait_recv()
            pass_on(c).wait_recv()
            block = rows[c].reshape(4 * lanes, width)
            depth = pl.ds(pl.multiple_of(c * width, width), width)
            acc_g[...] += dot(block, wg[depth, :])
            acc_u[...] += dot(block, wu[depth, :])

        return carry

    lax.fori_loop(0, n + 3, dispatch, 0)

    gate_out, up_out = acc_g[...], acc_u[...]
    hidden = gate_out / (1.0 + jnp.exp(-gate_out)) * up_out
    hid[...] = hidden.astype(jnp.bfloat16).reshape(hid.shape)
    for copy in weights[2:]:
        copy.wait()

    def sums_to_mate(c):
        return remote(send_c.at[c], recv_c.at[c], rc_s.at[c], rc_r.at[c], mate)

    def sums_to_opp(c):
        return remote(send_x.at[c], recv_x.at[c], rx_s.at[c], rx_r.at[c], opp)

    def combine(s, carry):
        @pl.when(s < n)
        def _():
            c = s
            for side in range(2):
                send_c[c, side] = dot(hid[side * 2 + (1 - core)], wd[c]).astype(jnp.bfloat16)
            sums_to_mate(c).start()

        @pl.when((s >= 1) & (s < n + 1))
        def _():
            c = s - 1
            sums_to_mate(c).wait_recv()
            total = dot(hid[opp_q], wd[c]) + recv_c[c, 1 - xl].astype(jnp.float32)
            send_x[c] = total.astype(jnp.bfloat16)
            sums_to_opp(c).start()

        @pl.when((s >= 2) & (s < n + 2))
        def _():
            c = s - 2
            sums_to_opp(c).wait_recv()
            total = (
                dot(hid[q], wd[c]) + recv_c[c, xl].astype(jnp.float32) + recv_x[c].astype(jnp.float32)
            )
            ret[c] = total.astype(jnp.bfloat16).reshape(js, zs * CAP, width)
            for device, there, _ in planes:
                remote(ret.at[c, there], retr.at[c, j], rp_s.at[c], rp_r.at[c], device).start()
            retr[c, j] = ret[c, j]

        @pl.when((s >= 3) & (s < n + 3))
        def _():
            c = s - 3
            wait_planes(retr, c, rp_s, rp_r).wait_recv()
            mixed = dot(mtbuf[...].reshape(zs * PAD, lanes), retr[c].reshape(lanes, width))
            zsend[c] = mixed.astype(jnp.bfloat16).reshape(zs, PAD, width)
            for device, there in columns:
                remote(zsend.at[c, there], zrecv.at[c, z], rz_s.at[c], rz_r.at[c], device).start()
            zrecv[c, z] = zsend[c, z]

        @pl.when(s >= 4)
        def _():
            c = s - 4
            wait_columns(zrecv, c, rz_s, rz_r).wait_recv()
            total = jnp.sum(zrecv[c].astype(jnp.float32), axis=0).astype(jnp.bfloat16)
            out_ref[:, pl.ds(pl.multiple_of(c * width, width), width)] = total[0:tok_rows]

        return carry

    lax.fori_loop(0, n + 4, combine, 0)

    remote(all_mts, all_mt, mt_sem.at[0], mt_sem.at[1], mate).wait_send()

    def finish(c, carry):
        wait_columns(zbuf, c, z_s, z_r).wait_send()
        wait_planes(slot, c, p_s, p_r).wait_send()
        to_mate(c).wait_send()
        to_opp(c).wait_send()
        pass_on(c).wait_send()
        sums_to_mate(c).wait_send()
        sums_to_opp(c).wait_send()
        wait_planes(ret, c, rp_s, rp_r).wait_send()
        wait_columns(zsend, c, rz_s, rz_r).wait_send()
        return carry

    lax.fori_loop(0, n, finish, 0)


def local(tokens, expert_ids, gates, w_gate, w_up, w_down):
    tok_rows, model_width = tokens.shape
    topk = expert_ids.shape[1]
    units = w_gate.shape[2]
    ys = YS
    js = 2 * ys
    zs = lax.axis_size("expert") // js
    width = min(CHUNK, model_width // 2)
    n = model_width // width
    lanes = js * zs * CAP
    held = zs * CAP
    bf = jnp.bfloat16
    vmem = pltpu.VMEM
    sems = lambda count: pltpu.SemaphoreType.DMA((count,))
    return pl.pallas_call(
        functools.partial(kernel, zs, ys, n, width),
        out_shape=jax.ShapeDtypeStruct((tok_rows, model_width), bf),
        in_specs=[pl.BlockSpec(memory_space=pltpu.VMEM)] * 3 + [pl.BlockSpec(memory_space=pl.ANY)] * 3,
        out_specs=pl.BlockSpec(memory_space=pltpu.VMEM),
        scratch_shapes=[
            vmem((PAD, topk), jnp.int32),
            vmem((PAD, topk), jnp.float32),
            vmem((zs, PAD, lanes), bf),
            vmem((zs, PAD, lanes), bf),
            vmem((lanes, zs * PAD), bf),
            vmem((n, zs, PAD, width), bf),
            vmem((n, js, held, width), bf),
            vmem((n, 4, js, held, width), bf),
            vmem((model_width, units), bf),
            vmem((model_width, units), bf),
            vmem((n, units, width), bf),
            vmem((4 * lanes, units), jnp.float32),
            vmem((4 * lanes, units), jnp.float32),
            vmem((4, lanes, units), bf),
            vmem((n, 2, lanes, width), bf),
            vmem((n, 2, lanes, width), bf),
            vmem((n, lanes, width), bf),
            vmem((n, lanes, width), bf),
            vmem((n, js, held, width), bf),
            vmem((n, js, held, width), bf),
            vmem((n, zs, PAD, width), bf),
            vmem((n, zs, PAD, width), bf),
            sems(2 + n),
            sems(2),
        ] + [sems(n)] * 18,
        compiler_params=pltpu.CompilerParams(
            collective_id=0, has_side_effects=True, vmem_limit_bytes=60 * 1024 * 1024
        ),
        cost_estimate=pl.CostEstimate(
            flops=2 * 4 * lanes * model_width * units * 3,
            bytes_accessed=3 * model_width * units * 2,
            transcendentals=4 * lanes * units,
        ),
    )(tokens, expert_ids, gates, w_gate, w_up, w_down)


def solution(mesh):
    in_specs = (
        P(("expert", "dp"), None),
        P(("expert", "dp"), None),
        P(("expert", "dp"), None),
        P("expert", None, "dp"),
        P("expert", None, "dp"),
        P("expert", "dp", None),
    )
    out_specs = P(("expert", "dp"), None)
    return jax.shard_map(local, mesh=mesh, in_specs=in_specs, out_specs=out_specs, check_vma=False)
```

time: 414 us -> 133 us (0.32)
  blocking collectives: 224 us -> 0 us
  waiting for transfers between devices: 147 us -> 0 us
  Pallas kernels: 0 us -> 126 us
  matrix products: 24.6 us -> 0 us
  starting transfers between devices: 10.5 us -> 0 us
    all_to_all x1 -> x0, blocking collectives: 178 us -> none  [local(): lax.all_to_all(outbound, 'expert', split_axis=0, concat_axis=0, tiled=True)]
    all_to_all x1 -> x0, waiting for transfers between devices: 142 us -> none  [local(): lax.all_to_all(jnp.einsum('senh,ehd->send', hidden, w_down, preferred_ele...]
    pallas_call x0 -> x1, Pallas kernels: none -> 126 us  [local(): pl.pallas_call(functools.partial(kernel, zs, ys, n, width), out_shape=jax...]
    all_gather x3 -> x0, blocking collectives: 33.9 us -> none  [the longest x1 19 us: local(): lax.all_gather(gates, 'dp', axis=0, tiled=True)]
    dot_general x4 -> x0, matrix products: 24.6 us -> none  [the longest x1 15.9 us: local(): jnp.einsum('senh,ehd->send', hidden, w_down, preferred_element_type=jnp.f...]
    unnamed x1 -> x0, blocking collectives: 12.5 us -> none
    all_to_all x1 -> x0, starting transfers between devices: 8.62 us -> none  [local(): lax.all_to_all(jnp.einsum('senh,ehd->send', hidden, w_down, preferred_ele...]
    unnamed x1 -> x0, waiting for transfers between devices: 4.16 us -> none
  transfers between devices with their start and end apart: 2 -> 0, of which waited for: 2 -> 0; matrix products, arithmetic and copies ran while one was open for 0% -> 0% of each run, Pallas kernels for 0% -> 0%
where the time goes in v1:
time: 133 us; the launch traced here: 131 us
  Pallas kernels  126 us (95%)
  local copies, waits for them, and re-layouts  4.35 us (3%)
    pallas_call x1, Pallas kernels, local(): pl.pallas_call(functools.partial(kernel, zs, ys, n, width), out_shape=jax...  126 us
    unnamed x3, local copies, waits for them, and re-layouts  4.35 us

profile of v1, /device:TPU:6, one launch (start us, length us, event | category | flops | bytes accessed | tf_op | source)
XLA Modules:
  0.0 130.7 jit_solution(677774371666988672)
XLA Ops:
  0.0 1.4 %copy.8.gates_ref = bf16[12,8]{1,0:T(8,128)(2,1)} copy(bf16[12,8]{0,1:T(8,128)(2,1)} %param.8) | data formatting | bytes 384 | tf_op args[2]
  1.4 1.4 %copy.7.ids_ref = s32[12,8]{1,0:T(8,128)} copy(s32[12,8]{0,1:T(8,128)} %param.7) | data formatting | bytes 768 | tf_op args[1]
  2.7 126.4 %shard_map.64 = bf16[12,7168]{1,0:T(8,128)(2,1)} custom-call(bf16[12,7168]{1,0:T(8,128)(2,1)} %tok_ref.1, s32[12,8]{1,0:T(8,128)} %copy.7.ids_ref, bf16[12,8]{1,0:T(8,128)(2,1)} %copy.8.gates_ref, bf16[1,7168,256]{2,1,0:T(8,128)(2,1)} %wg_hbm.1, bf16[1,7168,256]{2,1,0:T(8,128)(2,1)} %wu_hbm.1, bf16[1,256,7168]{2,1,0:T(8,128)(2,1)} %wd_hbm.1), custom_call_target="tpu_custom_call" | custom-call | flops 5637144576 | bytes 11010048 | tf_op jit(solution)/shard_map/pallas_call | solution.py:272
  129.1 1.6 %copy.10 = bf16[12,7168]{1,0:T(8,128)(2,1)} copy(bf16[12,7168]{1,0:T(8,128)(2,1)} %shard_map.64) | data formatting | bytes 344064

commit v2 on v1

v2 whole, which is shorter than its diff:
```python
import functools

import jax
import jax.numpy as jnp
from jax import lax
from jax.experimental import pallas as pl
from jax.experimental.pallas import tpu as pltpu
from jax.sharding import PartitionSpec as P

CAP = 2
PAD = 16
YS = 4
CHUNK = 1024
KINDS = "aababab"
ORDER_OUT = (0, 1, 2, 3, 4, 5, 6)
ORDER_BACK = (6, 5, 4, 3, 2, 1, 0)
PACE_OUT = 1.2
PACE_BACK = 1.2
MESH = pl.DeviceIdType.MESH


def dot(a, b):
    return jnp.dot(a, b, preferred_element_type=jnp.float32)


def kernel(
    zs, ys, n, width,
    tok_ref, ids_ref, gates_ref, wg_hbm, wu_hbm, wd_hbm, out_ref,
    flip_i, flip_g, mtsend, mtbuf, mtopp, sel, zbuf, slot, rows, wg, wu, wd, acc_g, acc_u, hid,
    send_c, recv_c, send_x, recv_x, ret, retr, zsend, zrecv, last_s, last_r,
    w_sem, mt_sem, x_s, x_r, z_s, z_r, p_s, p_r, o_s, o_r, k_s, k_r,
    rc_s, rc_r, rx_s, rx_r, rp_s, rp_r, rz_s, rz_r, rl_s, rl_r,
):
    e = lax.axis_index("expert")
    q = lax.axis_index("dp")
    js = 2 * ys
    z, j = e // js, e % js
    y, xh = j // 2, j % 2
    xl, core = q // 2, q % 2
    topk, tok_rows = ids_ref.shape
    held = zs * CAP
    lanes = js * held
    kinds = [KINDS[c % len(KINDS)] for c in range(n)]

    planes = []
    for dy in range(ys):
        for dx in range(2):
            if dy or dx:
                there = ((y + dy) % ys) * 2 + (xh + dx) % 2
                side = xl if dx == 0 else 1 - xl
                planes.append(((z * js + there, side * 2 + core), there, side))
    columns = []
    for dz in range(1, zs):
        there = (z + dz) % zs
        columns.append(((there * js + j, q), there))
    long_hops, short_hops = zs // 2, zs - 1 - zs // 2
    step = 1 + core * (zs - 2)

    def at_z(hops, sign):
        return (z + zs * zs + sign * hops * step) % zs

    ahead, behind = (at_z(1, 1) * js + j, q), (at_z(1, -1) * js + j, q)
    mate = (e, xl * 2 + (1 - core))
    opp = (e, (1 - xl) * 2 + core)

    barrier = pltpu.get_barrier_semaphore()
    partners = [p[0] for p in planes] + [c[0] for c in columns] + [mate, opp]
    for partner in partners:
        pl.semaphore_signal(barrier, inc=1, device_id=partner, device_id_type=MESH)

    weights = [
        pltpu.make_async_copy(wg_hbm.at[0], wg, w_sem.at[0]),
        pltpu.make_async_copy(wu_hbm.at[0], wu, w_sem.at[1]),
    ] + [
        pltpu.make_async_copy(wd_hbm.at[0, :, pl.ds(c * width, width)], wd.at[c], w_sem.at[2 + c])
        for c in range(n)
    ]
    for copy in weights:
        copy.start()

    def remote(src, dst, send, recv, device):
        return pltpu.make_async_remote_copy(
            src_ref=src, dst_ref=dst, send_sem=send, recv_sem=recv,
            device_id=device, device_id_type=MESH,
        )

    for c in range(n):
        zbuf[c, z, 0] = jnp.zeros((PAD, width), jnp.bfloat16)
        zbuf[c, z, 0, 0:tok_rows, :] = tok_ref[:, c * width:(c + 1) * width]

    flip_i[...] = jnp.full(flip_i.shape, -1.0, jnp.float32)
    flip_i[0:topk, 0:tok_rows] = ids_ref[...].astype(jnp.float32)
    flip_g[...] = jnp.zeros(flip_g.shape, jnp.float32)
    flip_g[0:topk, 0:tok_rows] = gates_ref[...].astype(jnp.float32)
    ids = flip_i[...].T[0:PAD]
    gates = flip_g[...].T[0:PAD]
    lane = lax.broadcasted_iota(jnp.int32, (PAD, lanes), 1)
    lane_expert = lane // held
    lane_mine = (lane // CAP) % zs == z
    lane_slot = (lane % CAP).astype(jnp.float32)
    lower = (
        lax.broadcasted_iota(jnp.int32, (PAD, PAD), 0) > lax.broadcasted_iota(jnp.int32, (PAD, PAD), 1)
    ).astype(jnp.float32)
    for plane in range(zs):
        named = jnp.zeros((PAD, lanes), jnp.float32)
        weight = jnp.zeros((PAD, lanes), jnp.float32)
        for k in range(topk):
            match = ids[:, k:k + 1] == (lane_expert + plane * js).astype(jnp.float32)
            named = named + jnp.where(match, 1.0, 0.0)
            weight = weight + jnp.where(match, gates[:, k:k + 1], 0.0)
        before = dot(lower, named)
        mtsend[plane] = jnp.where((before == lane_slot) & lane_mine, weight, 0.0).astype(jnp.bfloat16)
    mtbuf[z] = mtsend[z]

    pl.semaphore_wait(barrier, len(partners))

    def sides(c):
        return 2 if kinds[c] == "b" else 1

    def swap_tokens(c):
        return remote(zbuf.at[c, z, 0], zbuf.at[c, z, 1], x_s.at[c], x_r.at[c], opp)

    def column_copy(c, origin, way, hop):
        part = zbuf.at[c, origin] if kinds[c] == "b" else zbuf.at[c, origin, 0]
        return remote(part, part, z_s.at[c], z_r.at[c, way * 4 + hop - 1], ahead if way == 0 else behind)

    def column_send(c, hop):
        if hop == 1:
            if kinds[c] == "b":
                swap_tokens(c).wait_recv()
            column_copy(c, z, 0, 1).start()
            column_copy(c, z, 1, 1).start()
            return
        if hop <= long_hops:
            column_copy(c, at_z(hop - 1, -1), 0, hop - 1).wait_recv()
            column_copy(c, at_z(hop - 1, -1), 0, hop).start()
        if hop <= short_hops:
            column_copy(c, at_z(hop - 1, 1), 1, hop - 1).wait_recv()
            column_copy(c, at_z(hop - 1, 1), 1, hop).start()

    def plane_send(c):
        column_copy(c, at_z(long_hops, -1), 0, long_hops).wait_recv()
        if short_hops:
            column_copy(c, at_z(short_hops, 1), 1, short_hops).wait_recv()
        for side in range(sides(c)):
            chosen = dot(sel[side], zbuf[c, :, side].reshape(zs * PAD, width)).astype(jnp.bfloat16)
            chosen = chosen.reshape(js, held, width)
            if kinds[c] == "a":
                slot[c, 0] = chosen
            else:
                for there in range(js):
                    slot[c, (xl + side + xh + there) % 2, there] = chosen[there]
        for device, there, dest in planes:
            for side in range(sides(c)):
                group = dest if kinds[c] == "a" else side
                src, dst = slot.at[c, side, there], rows.at[c, core, group, j]
                remote(src, dst, p_s.at[c], p_r.at[c], device).start()
        if kinds[c] == "a":
            rows[c, core, xl, j] = slot[c, 0, j]
        else:
            for side in range(2):
                rows[c, core, side, j] = slot[c, side, j]

    def plane_wait(buf, c, send, recv):
        part = buf.at[c, pl.ds(0, sides(c)), pl.ds(0, js - 1)]
        return remote(part, part, send.at[c], recv.at[c], mate)

    def to_opp(c):
        part = rows.at[c, core, xl]
        return remote(part, part, o_s.at[c], o_r.at[c], opp)

    def to_mate(c):
        part = rows.at[c, core]
        return remote(part, part, k_s.at[c], k_r.at[c], mate)

    def opp_send(c):
        plane_wait(slot, c, p_s, p_r).wait_recv()
        to_opp(c).start()

    def mate_send(c):
        if kinds[c] == "a":
            to_opp(c).wait_recv()
        else:
            plane_wait(slot, c, p_s, p_r).wait_recv()
        to_mate(c).start()

    multiplied = []

    def multiply(c):
        first = not multiplied
        multiplied.append(c)
        to_mate(c).wait_recv()
        if first:
            weights[0].wait()
            weights[1].wait()
        block = rows[c].reshape(4 * lanes, width)
        gate_part = dot(block, wg[c * width:(c + 1) * width, :])
        up_part = dot(block, wu[c * width:(c + 1) * width, :])
        acc_g[...] = gate_part if first else acc_g[...] + gate_part
        acc_u[...] = up_part if first else acc_u[...] + up_part

    def routes_out():
        for device, there in columns:
            remote(mtsend.at[there], mtbuf.at[z], mt_sem.at[0], mt_sem.at[1], device).start()

    def routes_wait():
        return remote(
            mtsend.at[pl.ds(0, zs - 1)], mtbuf.at[pl.ds(0, zs - 1)], mt_sem.at[0], mt_sem.at[1], mate
        )

    def routes_to_opp():
        return remote(mtbuf, mtopp, mt_sem.at[2], mt_sem.at[3], opp)

    def selection(buf):
        values = buf[...].reshape(zs * PAD, lanes).astype(jnp.float32)
        return jnp.where(values != 0.0, 1.0, 0.0).T.astype(jnp.bfloat16)

    def choose_own():
        routes_wait().wait_recv()
        routes_to_opp().start()
        sel[0] = selection(mtbuf)

    def choose_opp():
        routes_to_opp().wait_recv()
        sel[1] = selection(mtopp)

    both = [c for c in range(n) if kinds[c] == "b"]
    for c in both:
        swap_tokens(c).start()
    routes_out()
    tasks = []
    for place in range(n):
        c = [v for v in ORDER_OUT if v < n][place]
        at = place * PACE_OUT
        for hop in range(1, long_hops + 1):
            tasks.append((at + 1.6 * (hop - 1) - (2.0 if hop == 1 else 0.0), functools.partial(column_send, c, hop)))
        at += 1.6 * long_hops
        tasks.append((at, functools.partial(plane_send, c)))
        if kinds[c] == "a":
            tasks.append((at + 4.0, functools.partial(opp_send, c)))
            tasks.append((at + 11.0, functools.partial(mate_send, c)))
            at += 13.5
        else:
            tasks.append((at + 7.5, functools.partial(mate_send, c)))
            at += 10.0
        tasks.append((at, functools.partial(multiply, c)))
    tasks.append((1.5, choose_own))
    tasks.append((4.5, choose_opp))
    for _, task in sorted(tasks, key=lambda pair: pair[0]):
        task()

    gate_out, up_out = acc_g[...], acc_u[...]
    hidden = gate_out / (1.0 + jnp.exp(-gate_out)) * up_out
    hid[...] = hidden.astype(jnp.bfloat16).reshape(hid.shape)
    for copy in weights[2:]:
        copy.wait()

    def sums_to_mate(c):
        return remote(send_c.at[c], recv_c.at[c], rc_s.at[c], rc_r.at[c], mate)

    def sums_to_opp(c):
        return remote(send_x.at[c], recv_x.at[c], rx_s.at[c], rx_r.at[c], opp)

    def core_sums(c):
        block = hid[1 - core].reshape(2 * lanes, hid.shape[-1])
        send_c[c] = dot(block, wd[c]).astype(jnp.bfloat16).reshape(2, lanes, width)
        sums_to_mate(c).start()

    def chip_sums(c):
        sums_to_mate(c).wait_recv()
        total = dot(hid[core, 1 - xl], wd[c]) + recv_c[c, 1 - xl].astype(jnp.float32)
        send_x[c] = total.astype(jnp.bfloat16)
        sums_to_opp(c).start()

    def plane_return(c):
        if kinds[c] == "a":
            sums_to_opp(c).wait_recv()
            total = (
                dot(hid[core, xl], wd[c])
                + recv_c[c, xl].astype(jnp.float32)
                + recv_x[c].astype(jnp.float32)
            )
            ret[c, 0] = total.astype(jnp.bfloat16).reshape(js, held, width)
        else:
            sums_to_mate(c).wait_recv()
            for side in range(2):
                total = dot(hid[core, side], wd[c]) + recv_c[c, side].astype(jnp.float32)
                ret[c, side] = total.astype(jnp.bfloat16).reshape(js, held, width)
        for device, there, _ in planes:
            for side in range(sides(c)):
                src, dst = ret.at[c, side, there], retr.at[c, side, j]
                remote(src, dst, rp_s.at[c], rp_r.at[c], device).start()
        for side in range(sides(c)):
            retr[c, side, j] = ret[c, side, j]

    def return_copy(c, target, way, hop):
        src, dst = zsend.at[c, target], zrecv.at[c, way * 4 + hop - 1]
        if kinds[c] == "a":
            src, dst = src.at[0], dst.at[0]
        return remote(
            src, dst,
            rz_s.at[c], rz_r.at[c, way * 4 + hop - 1], ahead if way == 0 else behind,
        )

    def token_sums(c):
        plane_wait(retr, c, rp_s, rp_r).wait_recv()
        for side in range(sides(c)):
            if kinds[c] == "a":
                block = retr[c, 0].reshape(lanes, width)
            else:
                block = jnp.concatenate(
                    [retr[c, (xl + side + xh + there) % 2, there] for there in range(js)], axis=0
                )
            mixing = (mtbuf if side == 0 else mtopp)[...].reshape(zs * PAD, lanes)
            zsend[c, :, side] = dot(mixing, block).astype(jnp.bfloat16).reshape(zs, PAD, width)
        return_copy(c, at_z(long_hops, 1), 0, 1).start()

    def add_in(c, target, way, hop):
        for side in range(sides(c)):
            total = zsend[c, target, side].astype(jnp.float32)
            total = total + zrecv[c, way * 4 + hop - 1, side].astype(jnp.float32)
            zsend[c, target, side] = total.astype(jnp.bfloat16)

    def return_send(c, hop):
        target = at_z(long_hops - hop + 1, 1)
        return_copy(c, target, 0, hop - 1).wait_recv()
        add_in(c, target, 0, hop - 1)
        return_copy(c, target, 0, hop).start()
        hop = hop - (long_hops - short_hops)
        if hop >= 1:
            target = at_z(short_hops - hop + 1, -1)
            if hop >= 2:
                return_copy(c, target, 1, hop - 1).wait_recv()
                add_in(c, target, 1, hop - 1)
            return_copy(c, target, 1, hop).start()

    def column_total(c, side):
        total = zsend[c, z, side].astype(jnp.float32)
        total = total + zrecv[c, long_hops - 1, side].astype(jnp.float32)
        if short_hops:
            total = total + zrecv[c, 4 + short_hops - 1, side].astype(jnp.float32)
        return total

    def swap_sums(c):
        return remote(last_s.at[c], last_r.at[c], rl_s.at[c], rl_r.at[c], opp)

    def columns_done(c):
        return_copy(c, z, 0, long_hops).wait_recv()
        if short_hops:
            return_copy(c, z, 1, short_hops).wait_recv()
        if kinds[c] == "b":
            last_s[c] = column_total(c, 1).astype(jnp.bfloat16)
            swap_sums(c).start()
        else:
            out_ref[:, c * width:(c + 1) * width] = column_total(c, 0).astype(jnp.bfloat16)[0:tok_rows]

    def finish(c):
        swap_sums(c).wait_recv()
        total = column_total(c, 0) + last_r[c].astype(jnp.float32)
        out_ref[:, c * width:(c + 1) * width] = total.astype(jnp.bfloat16)[0:tok_rows]

    tasks = []
    for place in range(n):
        c = [v for v in ORDER_BACK if v < n][place]
        at = place * PACE_BACK
        tasks.append((at, functools.partial(core_sums, c)))
        if kinds[c] == "a":
            tasks.append((at + 2.5, functools.partial(chip_sums, c)))
            tasks.append((at + 9.5, functools.partial(plane_return, c)))
            at += 14.0
        else:
            tasks.append((at + 2.5, functools.partial(plane_return, c)))
            at += 10.0
        tasks.append((at, functools.partial(token_sums, c)))
        for hop in range(2, long_hops + 1):
            tasks.append((at + 1.6 * (hop - 1), functools.partial(return_send, c, hop)))
        at += 1.6 * long_hops
        tasks.append((at, functools.partial(columns_done, c)))
        if kinds[c] == "b":
            tasks.append((at + 2.0, functools.partial(finish, c)))
    for _, task in sorted(tasks, key=lambda pair: pair[0]):
        task()

    routes_wait().wait_send()
    routes_to_opp().wait_send()
    for c in range(n):
        if kinds[c] == "b":
            swap_tokens(c).wait_send()
            swap_sums(c).wait_send()
        else:
            to_opp(c).wait_send()
            sums_to_opp(c).wait_send()
        part = zbuf.at[c, pl.ds(0, zs - 1), pl.ds(0, sides(c))]
        remote(part, part, z_s.at[c], z_r.at[c, 0], mate).wait_send()
        plane_wait(slot, c, p_s, p_r).wait_send()
        to_mate(c).wait_send()
        sums_to_mate(c).wait_send()
        plane_wait(ret, c, rp_s, rp_r).wait_send()
        part = zsend.at[c, pl.ds(0, zs - 1), pl.ds(0, sides(c))]
        remote(part, part, rz_s.at[c], rz_r.at[c, 0], mate).wait_send()


def local(tokens, expert_ids, gates, w_gate, w_up, w_down):
    tok_rows, model_width = tokens.shape
    units = w_gate.shape[2]
    ys = YS
    js = 2 * ys
    zs = lax.axis_size("expert") // js
    width = min(CHUNK, model_width // 2)
    n = model_width // width
    held = zs * CAP
    lanes = js * held
    bf = jnp.bfloat16
    vmem = pltpu.VMEM
    sems = lambda *shape: pltpu.SemaphoreType.DMA(shape)
    return pl.pallas_call(
        functools.partial(kernel, zs, ys, n, width),
        out_shape=jax.ShapeDtypeStruct((tok_rows, model_width), bf),
        in_specs=[pl.BlockSpec(memory_space=pltpu.VMEM)] * 3 + [pl.BlockSpec(memory_space=pl.ANY)] * 3,
        out_specs=pl.BlockSpec(memory_space=pltpu.VMEM),
        scratch_shapes=[
            vmem((128, 128), jnp.float32),
            vmem((128, 128), jnp.float32),
            vmem((zs, PAD, lanes), bf),
            vmem((zs, PAD, lanes), bf),
            vmem((zs, PAD, lanes), bf),
            vmem((2, lanes, zs * PAD), bf),
            vmem((n, zs, 2, PAD, width), bf),
            vmem((n, 2, js, held, width), bf),
            vmem((n, 2, 2, js, held, width), bf),
            vmem((model_width, units), bf),
            vmem((model_width, units), bf),
            vmem((n, units, width), bf),
            vmem((4 * lanes, units), jnp.float32),
            vmem((4 * lanes, units), jnp.float32),
            vmem((2, 2, lanes, units), bf),
            vmem((n, 2, lanes, width), bf),
            vmem((n, 2, lanes, width), bf),
            vmem((n, lanes, width), bf),
            vmem((n, lanes, width), bf),
            vmem((n, 2, js, held, width), bf),
            vmem((n, 2, js, held, width), bf),
            vmem((n, zs, 2, PAD, width), bf),
            vmem((n, 8, 2, PAD, width), bf),
            vmem((n, PAD, width), bf),
            vmem((n, PAD, width), bf),
            sems(2 + n), sems(4),
            sems(n), sems(n),
            sems(n), sems(n, 8),
            sems(n), sems(n), sems(n), sems(n), sems(n), sems(n),
            sems(n), sems(n), sems(n), sems(n), sems(n), sems(n),
            sems(n), sems(n, 8),
            sems(n), sems(n),
        ],
        compiler_params=pltpu.CompilerParams(
            collective_id=0, has_side_effects=True, vmem_limit_bytes=62 * 1024 * 1024
        ),
        cost_estimate=pl.CostEstimate(
            flops=2 * 4 * lanes * model_width * units * 3,
            bytes_accessed=3 * model_width * units * 2,
            transcendentals=4 * lanes * units,
        ),
    )(tokens, expert_ids.T, gates.T, w_gate, w_up, w_down)


def solution(mesh):
    in_specs = (
        P(("expert", "dp"), None),
        P(("expert", "dp"), None),
        P(("expert", "dp"), None),
        P("expert", None, "dp"),
        P("expert", None, "dp"),
        P("expert", "dp", None),
    )
    out_specs = P(("expert", "dp"), None)
    return jax.shard_map(local, mesh=mesh, in_specs=in_specs, out_specs=out_specs, check_vma=False)
```

time: 133 us -> 118 us (0.89)
  Pallas kernels: 126 us -> 115 us
  local copies, waits for them, and re-layouts: 4.35 us -> 1.64 us
    pallas_call x1, Pallas kernels: 126 us -> 115 us  [local(): pl.pallas_call(functools.partial(kernel, zs, ys, n, width), out_shape=jax...]
    unnamed x3 -> x1, local copies, waits for them, and re-layouts: 4.35 us -> 1.64 us
where the time goes in v2:
time: 118 us; the launch traced here: 117 us
  Pallas kernels  115 us (97%)
  local copies, waits for them, and re-layouts  1.64 us (1%)
    pallas_call x1, Pallas kernels, local(): pl.pallas_call(functools.partial(kernel, zs, ys, n, width), out_shape=jax...  115 us

profile of v2, /device:TPU:6, one launch (start us, length us, event | category | flops | bytes accessed | tf_op | source)
XLA Modules:
  0.0 116.6 jit_solution(11691176160880410302)
XLA Ops:
  0.0 115.0 %shard_map.64 = bf16[12,7168]{1,0:T(8,128)(2,1)} custom-call(bf16[12,7168]{1,0:T(8,128)(2,1)} %tok_ref.1, s32[8,12]{1,0:T(8,128)} %bitcast.2, bf16[8,12]{1,0:T(8,128)(2,1)} %bitcast.3, bf16[1,7168,256]{2,1,0:T(8,128)(2,1)} %wg_hbm.1, bf16[1,7168,256]{2,1,0:T(8,128)(2,1)} %wu_hbm.1, bf16[1,256,7168]{2,1,0:T(8,128)(2,1)} %wd_hbm.1), custom_call_target="tpu_custom_call" | custom-call | flops 5637144576 | bytes 11010048 | tf_op jit(solution)/shard_map/pallas_call | solution.py:416
  115.0 1.6 %copy.8 = bf16[12,7168]{1,0:T(8,128)(2,1)} copy(bf16[12,7168]{1,0:T(8,128)(2,1)} %shard_map.64) | data formatting | bytes 344064

commit v3 on v2

--- a/solution.py
+++ b/solution.py
@@ -11,11 +11,17 @@
 PAD = 16
 YS = 4
 CHUNK = 1024
-KINDS = "aababab"
-ORDER_OUT = (0, 1, 2, 3, 4, 5, 6)
-ORDER_BACK = (6, 5, 4, 3, 2, 1, 0)
-PACE_OUT = 1.2
-PACE_BACK = 1.2
+KINDS = "abababa"
+ORDER_OUT = (
+    14, 12, 10, 22, 8, 20, 18, 30, 9, 28, 38, 26, 16, 17, 36, 13, 46, 24, 34, 11, 25, 44, 32, 21, 42,
+    54, 33, 40, 29, 19, 52, 41, 37, 62, 50, 27, 45, 48, 35, 57, 43, 60, 61, 65, 58, 68, 70, 56, 69, 59,
+    66, 64, 67,
+)
+ORDER_BACK = (
+    3, 4, 6, 1, 19, 12, 2, 5, 14, 0, 17, 21, 10, 27, 35, 25, 8, 20, 43, 33, 22, 29, 51, 18, 41, 37, 28,
+    16, 30, 49, 45, 26, 36, 57, 38, 24, 34, 53, 32, 44, 46, 59, 42, 65, 40, 52, 54, 61, 50, 67, 48, 58,
+    62, 69, 60, 56,
+)
 MESH = pl.DeviceIdType.MESH
 
 
@@ -94,22 +100,23 @@
     flip_g[0:topk, 0:tok_rows] = gates_ref[...].astype(jnp.float32)
     ids = flip_i[...].T[0:PAD]
     gates = flip_g[...].T[0:PAD]
-    lane = lax.broadcasted_iota(jnp.int32, (PAD, lanes), 1)
-    lane_expert = lane // held
-    lane_mine = (lane // CAP) % zs == z
+    lane = lax.broadcasted_iota(jnp.int32, (PAD, zs * lanes), 1)
+    lane_expert = (lane // held).astype(jnp.float32)
     lane_slot = (lane % CAP).astype(jnp.float32)
     lower = (
         lax.broadcasted_iota(jnp.int32, (PAD, PAD), 0) > lax.broadcasted_iota(jnp.int32, (PAD, PAD), 1)
-    ).astype(jnp.float32)
+    ).astype(jnp.bfloat16)
+    named = jnp.zeros(lane.shape, jnp.float32)
+    weight = jnp.zeros(lane.shape, jnp.float32)
+    for k in range(topk):
+        match = ids[:, k:k + 1] == lane_expert
+        named = named + jnp.where(match, 1.0, 0.0)
+        weight = weight + jnp.where(match, gates[:, k:k + 1], 0.0)
+    before = dot(lower, named.astype(jnp.bfloat16))
+    mine = (before == lane_slot) & ((lane // CAP) % zs == z)
+    routed = jnp.where(mine, weight, 0.0).astype(jnp.bfloat16)
     for plane in range(zs):
-        named = jnp.zeros((PAD, lanes), jnp.float32)
-        weight = jnp.zeros((PAD, lanes), jnp.float32)
-        for k in range(topk):
-            match = ids[:, k:k + 1] == (lane_expert + plane * js).astype(jnp.float32)
-            named = named + jnp.where(match, 1.0, 0.0)
-            weight = weight + jnp.where(match, gates[:, k:k + 1], 0.0)
-        before = dot(lower, named)
-        mtsend[plane] = jnp.where((before == lane_slot) & lane_mine, weight, 0.0).astype(jnp.bfloat16)
+        mtsend[plane] = routed[:, plane * lanes:(plane + 1) * lanes]
     mtbuf[z] = mtsend[z]
 
     pl.semaphore_wait(barrier, len(partners))
@@ -228,26 +235,18 @@
     for c in both:
         swap_tokens(c).start()
     routes_out()
-    tasks = []
-    for place in range(n):
-        c = [v for v in ORDER_OUT if v < n][place]
-        at = place * PACE_OUT
-        for hop in range(1, long_hops + 1):
-            tasks.append((at + 1.6 * (hop - 1) - (2.0 if hop == 1 else 0.0), functools.partial(column_send, c, hop)))
-        at += 1.6 * long_hops
-        tasks.append((at, functools.partial(plane_send, c)))
-        if kinds[c] == "a":
-            tasks.append((at + 4.0, functools.partial(opp_send, c)))
-            tasks.append((at + 11.0, functools.partial(mate_send, c)))
-            at += 13.5
-        else:
-            tasks.append((at + 7.5, functools.partial(mate_send, c)))
-            at += 10.0
-        tasks.append((at, functools.partial(multiply, c)))
-    tasks.append((1.5, choose_own))
-    tasks.append((4.5, choose_opp))
-    for _, task in sorted(tasks, key=lambda pair: pair[0]):
-        task()
+    hops = [functools.partial(column_send, hop=hop) for hop in range(1, 5)]
+    steps = [None] + hops + [plane_send, opp_send, mate_send, multiply]
+    chosen_own = chosen_opp = False
+    for code in ORDER_OUT:
+        number, c = code // 8, code % 8
+        if not chosen_own and number >= 4:
+            choose_own()
+            chosen_own = True
+        if not chosen_opp and number == 5 and kinds[c] == "b":
+            choose_opp()
+            chosen_opp = True
+        steps[number](c)
 
     gate_out, up_out = acc_g[...], acc_u[...]
     hidden = gate_out / (1.0 + jnp.exp(-gate_out)) * up_out
@@ -359,27 +358,10 @@
         total = column_total(c, 0) + last_r[c].astype(jnp.float32)
         out_ref[:, c * width:(c + 1) * width] = total.astype(jnp.bfloat16)[0:tok_rows]
 
-    tasks = []
-    for place in range(n):
-        c = [v for v in ORDER_BACK if v < n][place]
-        at = place * PACE_BACK
-        tasks.append((at, functools.partial(core_sums, c)))
-        if kinds[c] == "a":
-            tasks.append((at + 2.5, functools.partial(chip_sums, c)))
-            tasks.append((at + 9.5, functools.partial(plane_return, c)))
-            at += 14.0
-        else:
-            tasks.append((at + 2.5, functools.partial(plane_return, c)))
-            at += 10.0
-        tasks.append((at, functools.partial(token_sums, c)))
-        for hop in range(2, long_hops + 1):
-            tasks.append((at + 1.6 * (hop - 1), functools.partial(return_send, c, hop)))
-        at += 1.6 * long_hops
-        tasks.append((at, functools.partial(columns_done, c)))
-        if kinds[c] == "b":
-            tasks.append((at + 2.0, functools.partial(finish, c)))
-    for _, task in sorted(tasks, key=lambda pair: pair[0]):
-        task()
+    hops = [functools.partial(return_send, hop=hop) for hop in range(2, 5)]
+    steps = [core_sums, chip_sums, plane_return, token_sums] + hops + [columns_done, finish]
+    for code in ORDER_BACK:
+        steps[code // 8](code % 8)
 
     routes_wait().wait_send()
     routes_to_opp().wait_send()

time: 118 us -> 108 us (0.915); the launches traced: 117 us -> 108 us
  Pallas kernels: 115 us -> 106 us
    pallas_call x1, Pallas kernels: 115 us -> 106 us  [local(): pl.pallas_call(functools.partial(kernel, zs, ys, n, width), out_shape=jax...]
where the time goes in v3:
time: 108 us
  Pallas kernels  106 us (98%)
  local copies, waits for them, and re-layouts  1.64 us (2%)
    pallas_call x1, Pallas kernels, local(): pl.pallas_call(functools.partial(kernel, zs, ys, n, width), out_shape=jax...  106 us

profile of v3, /device:TPU:6, one launch (start us, length us, event | category | flops | bytes accessed | tf_op | source)
XLA Modules:
  0.0 107.9 jit_solution(12954156149544149356)
XLA Ops:
  0.0 106.3 %shard_map.64 = bf16[12,7168]{1,0:T(8,128)(2,1)} custom-call(bf16[12,7168]{1,0:T(8,128)(2,1)} %tok_ref.1, s32[8,12]{1,0:T(8,128)} %bitcast.2, bf16[8,12]{1,0:T(8,128)(2,1)} %bitcast.3, bf16[1,7168,256]{2,1,0:T(8,128)(2,1)} %wg_hbm.1, bf16[1,7168,256]{2,1,0:T(8,128)(2,1)} %wu_hbm.1, bf16[1,256,7168]{2,1,0:T(8,128)(2,1)} %wd_hbm.1), custom_call_target="tpu_custom_call" | custom-call | flops 5637144576 | bytes 11010048 | tf_op jit(solution)/shard_map/pallas_call | solution.py:398
  106.3 1.6 %copy.8 = bf16[12,7168]{1,0:T(8,128)(2,1)} copy(bf16[12,7168]{1,0:T(8,128)(2,1)} %shard_map.64) | data formatting | bytes 344064

commit v4 on v3

--- a/solution.py
+++ b/solution.py
@@ -93,31 +93,6 @@
     for c in range(n):
         zbuf[c, z, 0] = jnp.zeros((PAD, width), jnp.bfloat16)
         zbuf[c, z, 0, 0:tok_rows, :] = tok_ref[:, c * width:(c + 1) * width]
-
-    flip_i[...] = jnp.full(flip_i.shape, -1.0, jnp.float32)
-    flip_i[0:topk, 0:tok_rows] = ids_ref[...].astype(jnp.float32)
-    flip_g[...] = jnp.zeros(flip_g.shape, jnp.float32)
-    flip_g[0:topk, 0:tok_rows] = gates_ref[...].astype(jnp.float32)
-    ids = flip_i[...].T[0:PAD]
-    gates = flip_g[...].T[0:PAD]
-    lane = lax.broadcasted_iota(jnp.int32, (PAD, zs * lanes), 1)
-    lane_expert = (lane // held).astype(jnp.float32)
-    lane_slot = (lane % CAP).astype(jnp.float32)
-    lower = (
-        lax.broadcasted_iota(jnp.int32, (PAD, PAD), 0) > lax.broadcasted_iota(jnp.int32, (PAD, PAD), 1)
-    ).astype(jnp.bfloat16)
-    named = jnp.zeros(lane.shape, jnp.float32)
-    weight = jnp.zeros(lane.shape, jnp.float32)
-    for k in range(topk):
-        match = ids[:, k:k + 1] == lane_expert
-        named = named + jnp.where(match, 1.0, 0.0)
-        weight = weight + jnp.where(match, gates[:, k:k + 1], 0.0)
-    before = dot(lower, named.astype(jnp.bfloat16))
-    mine = (before == lane_slot) & ((lane // CAP) % zs == z)
-    routed = jnp.where(mine, weight, 0.0).astype(jnp.bfloat16)
-    for plane in range(zs):
-        mtsend[plane] = routed[:, plane * lanes:(plane + 1) * lanes]
-    mtbuf[z] = mtsend[z]
 
     pl.semaphore_wait(barrier, len(partners))
 
@@ -206,6 +181,32 @@
         acc_g[...] = gate_part if first else acc_g[...] + gate_part
         acc_u[...] = up_part if first else acc_u[...] + up_part
 
+    def make_routes():
+        flip_i[...] = jnp.full(flip_i.shape, -1.0, jnp.float32)
+        flip_i[0:topk, 0:tok_rows] = ids_ref[...].astype(jnp.float32)
+        flip_g[...] = jnp.zeros(flip_g.shape, jnp.float32)
+        flip_g[0:topk, 0:tok_rows] = gates_ref[...].astype(jnp.float32)
+        ids = flip_i[...].T[0:PAD]
+        gates = flip_g[...].T[0:PAD]
+        lane = lax.broadcasted_iota(jnp.int32, (PAD, zs * lanes), 1)
+        lane_expert = (lane // held).astype(jnp.float32)
+        lane_slot = (lane % CAP).astype(jnp.float32)
+        lower = (
+            lax.broadcasted_iota(jnp.int32, (PAD, PAD), 0) > lax.broadcasted_iota(jnp.int32, (PAD, PAD), 1)
+        ).astype(jnp.bfloat16)
+        named = jnp.zeros(lane.shape, jnp.float32)
+        weight = jnp.zeros(lane.shape, jnp.float32)
+        for k in range(topk):
+            match = ids[:, k:k + 1] == lane_expert
+            named = named + jnp.where(match, 1.0, 0.0)
+            weight = weight + jnp.where(match, gates[:, k:k + 1], 0.0)
+        before = dot(lower, named.astype(jnp.bfloat16))
+        mine = (before == lane_slot) & ((lane // CAP) % zs == z)
+        routed = jnp.where(mine, weight, 0.0).astype(jnp.bfloat16)
+        for plane in range(zs):
+            mtsend[plane] = routed[:, plane * lanes:(plane + 1) * lanes]
+        mtbuf[z] = mtsend[z]
+
     def routes_out():
         for device, there in columns:
             remote(mtsend.at[there], mtbuf.at[z], mt_sem.at[0], mt_sem.at[1], device).start()
@@ -234,12 +235,14 @@
     both = [c for c in range(n) if kinds[c] == "b"]
     for c in both:
         swap_tokens(c).start()
-    routes_out()
     hops = [functools.partial(column_send, hop=hop) for hop in range(1, 5)]
     steps = [None] + hops + [plane_send, opp_send, mate_send, multiply]
     chosen_own = chosen_opp = False
-    for code in ORDER_OUT:
+    for place, code in enumerate(ORDER_OUT):
         number, c = code // 8, code % 8
+        if place == 1:
+            make_routes()
+            routes_out()
         if not chosen_own and number >= 4:
             choose_own()
             chosen_own = True

time: 108 us -> 108 us (level)
  no operation moved by 1% of the time
where the time goes in v4:
time: 108 us
  Pallas kernels  106 us (98%)
  local copies, waits for them, and re-layouts  1.64 us (2%)
    pallas_call x1, Pallas kernels, local(): pl.pallas_call(functools.partial(kernel, zs, ys, n, width), out_shape=jax...  106 us

profile of v4, /device:TPU:6, one launch (start us, length us, event | category | flops | bytes accessed | tf_op | source)
XLA Modules:
  0.0 108.1 jit_solution(9051352344452344021)
XLA Ops:
  0.0 106.4 %shard_map.64 = bf16[12,7168]{1,0:T(8,128)(2,1)} custom-call(bf16[12,7168]{1,0:T(8,128)(2,1)} %tok_ref.1, s32[8,12]{1,0:T(8,128)} %bitcast.2, bf16[8,12]{1,0:T(8,128)(2,1)} %bitcast.3, bf16[1,7168,256]{2,1,0:T(8,128)(2,1)} %wg_hbm.1, bf16[1,7168,256]{2,1,0:T(8,128)(2,1)} %wu_hbm.1, bf16[1,256,7168]{2,1,0:T(8,128)(2,1)} %wd_hbm.1), custom_call_target="tpu_custom_call" | custom-call | flops 5637144576 | bytes 11010048 | tf_op jit(solution)/shard_map/pallas_call | solution.py:401
  106.4 1.6 %copy.8 = bf16[12,7168]{1,0:T(8,128)(2,1)} copy(bf16[12,7168]{1,0:T(8,128)(2,1)} %shard_map.64) | data formatting | bytes 344064
